TPU v7x, 32 devices: a whole 2x2x4 slice. The times are simulated.
32 devices in a mesh: dom: 8 (over y, x, core), head: 4 (over z).
Axes of the slice: x: 2, y: 2, z: 4, core: 2. Of those that a mesh axis runs over, the one named last changes fastest.
Arguments:
- queries: bfloat16 [4608, 2048], P(('dom', 'head')), may hold values from -8 to 8
- keys_in: bfloat16 [4608, 2048], P(('dom', 'head')), may hold values from -8 to 8
- values_in: bfloat16 [4608, 2048], P(('dom', 'head')), may hold values from -6 to 6
- grad_out: bfloat16 [4608, 2048], P(('dom', 'head')), may hold values from -6 to 6
- pos_bias: float32 [32, 64, 576], P('head'), may hold values from -4 to 4
- neighbours: int32 [72, 9], P('dom'), may hold values from 0 to 32, as said below
- send_block: int32 [8, 8, 3], P('dom'), may hold values from 0 to 8, as said below
- orient: int32 [8, 8], P('dom'), may hold values from 0 to 7
Outputs:
- grad_q: bfloat16 [4608, 2048], P(('dom', 'head'))
- grad_k: bfloat16 [4608, 2048], P(('dom', 'head'))
- grad_v: bfloat16 [4608, 2048], P(('dom', 'head'))
Inputs may be any that keep to these rules, and one draw needn't show every extreme that they name: `neighbours`: entry [d * 9 + b, j] names the j-th key block of query block b of domain d: e below 9 is the domain's own block e, and 9 + k * 3 + c is slot c of what domain d borrows from direction k. The 9 entries of a query block are distinct and name only live slots of send_block. `send_block`: entry [p, k, c] is the block that domain p lends in slot c to the domain d with nb(d, k) = p. The live slots of one entry [p, k] name distinct blocks; there are 3 of them for the four edge directions and one for the four corner directions, none where no such d exists; slots that are not live hold 0 and no neighbours entry names them.
All inputs are finite; a program needn't handle non-finite values.
Results may differ from a plain program's by a relative error of at most 0.025.
Values may be sent and summed in bfloat16 or wider, within the bound.
No kernel may reach another device: no remote copies, remote signals or barrier semaphores. Data moves between devices by JAX's collectives and lax.ppermute only.
A program may use at most 128 MiB of HBM per device.

v0:
```python
import jax
import jax.numpy as jnp
import numpy as np
from jax import lax
from jax.sharding import PartitionSpec as P

HD = 64
PATCH = 8
BT = 64
GRID_ROWS = 4
DIRS = 8
WIN = 9
WINK = 576
QB_DOM = 9
CAP = 3


OFFSET_LIST = [(-1, -1), (-1, 0), (-1, 1), (0, -1), (0, 1), (1, -1), (1, 0), (1, 1)]


def from_behind(value, axis, steps):
    count = lax.axis_size(axis)
    first, last = (max(0, -steps), min(count, count - steps))
    return lax.ppermute(value, axis, [(source, source + steps) for source in range(first, last)])


def patch_tables(patch_side):
    flat_index = np.arange(patch_side * patch_side)
    row_of = flat_index // patch_side
    col_of = flat_index % patch_side
    table_list = []
    for orient_id in range(8):
        row_new = patch_side - 1 - row_of if orient_id % 2 == 1 else row_of
        col_new = patch_side - 1 - col_of if orient_id // 2 % 2 == 1 else col_of
        mapped = (
            patch_side * col_new + row_new if orient_id >= 4 else patch_side * row_new + col_new
        )
        table_list.append(mapped)
    forward = np.stack(table_list).astype(np.int32)
    inverse = np.argsort(forward, axis=1).astype(np.int32)
    return (forward, inverse)


def per_device(queries, keys_in, values_in, grad_out, pos_bias, neighbours, send_block, orient):
    head_local = pos_bias.shape[0]
    score_scale = HD ** (-0.5)
    grid_cols = lax.axis_size("dom") // GRID_ROWS
    slot_total = QB_DOM + DIRS * CAP
    forward, inverse = patch_tables(PATCH)
    query_heads, key_heads, value_heads, grad_heads = (
        lax.all_to_all(queries, "head", split_axis=1, concat_axis=0, tiled=True),
        lax.all_to_all(keys_in, "head", split_axis=1, concat_axis=0, tiled=True),
        lax.all_to_all(values_in, "head", split_axis=1, concat_axis=0, tiled=True),
        lax.all_to_all(grad_out, "head", split_axis=1, concat_axis=0, tiled=True),
    )
    tokens_dom = query_heads.shape[0]

    def split_heads(matrix):
        return matrix.reshape(QB_DOM, BT, head_local, HD)

    own_pairs = jnp.concatenate([split_heads(key_heads), split_heads(value_heads)], axis=-1)
    own_sends = send_block[0].reshape(-1)
    outgoing = own_pairs[own_sends].reshape(DIRS, CAP, BT, head_local, 2 * HD)
    arrived_groups = [None] * DIRS
    for index, (row_step, col_step) in enumerate(OFFSET_LIST):
        arrived_groups[index] = from_behind(
            outgoing[index], "dom", -(row_step * grid_cols + col_step)
        )
    arrived = jnp.stack(arrived_groups).reshape(DIRS * CAP, BT, head_local, 2 * HD)
    turn_index = jnp.repeat(jnp.asarray(forward)[orient[0]], CAP, axis=0)
    oriented = jnp.take_along_axis(arrived, turn_index[:, :, None, None], axis=1)
    extended = jnp.concatenate([own_pairs, oriented], axis=0)
    near_ids = neighbours.reshape(-1)
    window = extended[near_ids].reshape(QB_DOM, WINK, head_local, 2 * HD)
    win_k = window[..., :HD]
    win_v = window[..., HD:]
    query_blk = split_heads(query_heads)
    grad_blk = split_heads(grad_heads)
    scores = (
        jnp.einsum("bthd,bkhd->bhtk", query_blk, win_k, preferred_element_type=jnp.float32)
        * score_scale
        + pos_bias[None]
    )
    row_top = jnp.max(scores, axis=-1, keepdims=True)
    exp_scores = jnp.exp(scores - row_top)
    probs = exp_scores / jnp.sum(exp_scores, axis=-1, keepdims=True)
    probs_half = probs.astype(jnp.bfloat16)
    dprobs = jnp.einsum("bthd,bkhd->bhtk", grad_blk, win_v, preferred_element_type=jnp.float32)
    row_delta = jnp.sum(probs_half.astype(jnp.float32) * dprobs, axis=-1, keepdims=True)
    dscores = (probs * (dprobs - row_delta)).astype(jnp.bfloat16)
    grad_q_blk = (
        jnp.einsum("bhtk,bkhd->bthd", dscores, win_k, preferred_element_type=jnp.float32)
        * score_scale
    )
    grad_q_loc = grad_q_blk.astype(jnp.bfloat16).reshape(tokens_dom, head_local * HD)
    grad_kw = (
        jnp.einsum("bhtk,bthd->bkhd", dscores, query_blk, preferred_element_type=jnp.float32)
        * score_scale
    )
    grad_vw = jnp.einsum(
        "bhtk,bthd->bkhd", probs_half, grad_blk, preferred_element_type=jnp.float32
    )
    window_grad = jnp.concatenate([grad_kw, grad_vw], axis=-1).reshape(
        QB_DOM * WIN, BT, head_local, 2 * HD
    )
    slot_grad = jax.ops.segment_sum(window_grad, near_ids, num_segments=slot_total)
    back_order = jnp.repeat(jnp.asarray(inverse)[orient[0]], CAP, axis=0)
    leaving = jnp.take_along_axis(slot_grad[QB_DOM:], back_order[:, :, None, None], axis=1)
    leaving = leaving.astype(jnp.bfloat16).reshape(DIRS, CAP, BT, head_local, 2 * HD)
    back_groups = [None] * DIRS
    for index, (row_step, col_step) in enumerate(OFFSET_LIST):
        back_groups[index] = from_behind(leaving[index], "dom", row_step * grid_cols + col_step)
    returned = (
        jnp.stack(back_groups).reshape(DIRS * CAP, BT, head_local, 2 * HD).astype(jnp.float32)
    )
    own_grad = slot_grad[:QB_DOM] + jax.ops.segment_sum(returned, own_sends, num_segments=QB_DOM)
    grad_k_loc = own_grad[..., :HD].astype(jnp.bfloat16).reshape(tokens_dom, head_local * HD)
    grad_v_loc = own_grad[..., HD:].astype(jnp.bfloat16).reshape(tokens_dom, head_local * HD)
    return (
        lax.all_to_all(grad_q_loc, "head", split_axis=0, concat_axis=1, tiled=True),
        lax.all_to_all(grad_k_loc, "head", split_axis=0, concat_axis=1, tiled=True),
        lax.all_to_all(grad_v_loc, "head", split_axis=0, concat_axis=1, tiled=True),
    )


def solution(mesh):
    return jax.shard_map(
        per_device,
        mesh=mesh,
        in_specs=(
            P(("dom", "head"), None),
            P(("dom", "head"), None),
            P(("dom", "head"), None),
            P(("dom", "head"), None),
            P("head", None, None),
            P("dom", None),
            P("dom", None, None),
            P("dom", None),
        ),
        out_specs=(P(("dom", "head"), None), P(("dom", "head"), None), P(("dom", "head"), None)),
        check_vma=False,
    )
```

profile of v0, /device:TPU:4, one launch (start us, length us, event | category | flops | bytes accessed | tf_op | source)
XLA Modules:
  0.0 464.7 jit_solution(8294139374084826504)
XLA Ops:
  2.7 5.0 %all-to-all-start.1 = ((bf16[144,4,512]{2,0,1:T(8,128)(2,1)}), bf16[144,4,512]{2,0,1:T(8,128)(2,1)S(1)}, u32[]{:S(2)}, u32[]{:S(2)}) async-start(bf16[144,4,512]{2,0,1:T(8,128)(2,1)} %bitcast.121), calls=%async_computation.1 | async-start | bytes 1179648 | tf_op jit(solution)/shard_map/all_to_all | solution.py:53
  9.6 14.0 %all-to-all-done.1 = bf16[144,4,512]{2,0,1:T(8,128)(2,1)S(1)} async-done(((bf16[144,4,512]{2,0,1:T(8,128)(2,1)}), bf16[144,4,512]{2,0,1:T(8,128)(2,1)S(1)}, u32[]{:S(2)}, u32[]{:S(2)}) %all-to-all-start.1) | async-done | bytes 589856 | tf_op jit(solution)/shard_map/all_to_all | solution.py:53
  23.6 3.5 all-to-all-start
  28.6 13.9 %all-to-all-done = bf16[144,4,512]{2,0,1:T(8,128)(2,1)S(1)} async-done(((bf16[144,4,512]{2,0,1:T(8,128)(2,1)}), bf16[144,4,512]{2,0,1:T(8,128)(2,1)S(1)}, u32[]{:S(2)}, u32[]{:S(2)}) %all-to-all-start) | async-done | bytes 589856 | tf_op jit(solution)/shard_map/all_to_all | solution.py:52
  42.4 3.5 all-to-all-start.2
  53.2 8.1 %all-to-all-done.2 = bf16[144,4,512]{2,0,1:T(8,128)(2,1)S(1)} async-done(((bf16[144,4,512]{2,0,1:T(8,128)(2,1)}), bf16[144,4,512]{2,0,1:T(8,128)(2,1)S(1)}, u32[]{:S(2)}, u32[]{:S(2)}) %all-to-all-start.2) | async-done | bytes 589856 | tf_op jit(solution)/shard_map/all_to_all | solution.py:51
  62.1 4.1 all-to-all-start.3
  66.9 2.8 gather_fusion.1
  69.7 3.6 fusion.26
  75.9 2.6 collective-permute-start.1
  83.0 4.5 collective-permute-start.4
  91.3 2.5 reshape.322
  93.8 2.6 copy.43
  96.3 3.9 collective-permute-done
  103.9 2.5 collective-permute-start.6
  118.7 3.0 collective-permute-done.7
  122.5 15.3 %gather_fusion.4 = bf16[1536,8,128]{2,1,0:T(8,128)(2,1)} fusion(bf16[24,64,8,128]{3,2,1,0:T(8,128)(2,1)} %bitcast.13, s32[1536]{0:T(1024)S(1)} %reshape.357), kind=kCustom, calls=%fused_computation.4 | custom fusion | bytes 6303744 | tf_op jit(solution)/shard_map/jit(take_along_axis)/gather | solution.py:71
  137.8 5.5 %broadcast_select_fusion = bf16[24,64,8,128]{3,2,1,0:T(8,128)(2,1)S(1)} fusion(bf16[24,64,8,128]{3,2,1,0:T(8,128)(2,1)} %bitcast.127, pred[24,64]{1,0:T(8,128)(4,1)} %compare_and_fusion.1), kind=kLoop, calls=%fused_computation.29 | loop fusion | flops 1572864 | bytes 6292992 | tf_op jit(solution)/shard_map/jit(take_along_axis)/select_n | solution.py:71
  143.3 2.7 pad_maximum_fusion.1
  146.0 8.7 %gather_fusion.2 = bf16[81,64,8,128]{3,2,1,0:T(8,128)(2,1)} fusion(bf16[33,64,8,128]{3,2,1,0:T(8,128)(2,1)} %pad_maximum_fusion.1, s32[1024]{0:T(1024)} %get-tuple-element.27), kind=kCustom, calls=%fused_computation.2 | custom fusion | bytes 21233988 | tf_op jit(solution)/shard_map/gather | solution.py:74
  154.7 17.1 %fusion.24 = (bf16[9,576,8,64]{3,2,1,0:T(8,128)(2,1)}, bf16[9,576,8,64]{3,2,1,0:T(8,128)(2,1)}) fusion(bf16[9,576,8,128]{3,2,1,0:T(8,128)(2,1)} %bitcast.123), kind=kLoop, calls=%fused_computation.77 | loop fusion | bytes 21233664 | tf_op jit(solution)/shard_map/slice | solution.py:76
  171.9 14.0 %copy.48 = bf16[9,576,8,64]{1,3,2,0:T(8,128)(2,1)} copy(bf16[9,576,8,64]{3,2,1,0:T(8,128)(2,1)} %get-tuple-element.4) | data formatting | bytes 10616832
  185.9 11.1 %fusion.28 = (f32[9,8,64]{2,1,0:T(8,128)S(1)}, f32[9,8,64,576]{3,2,1,0:T(8,128)}) fusion(f32[8,64,576]{2,1,0:T(8,128)S(1)} %copy-done.4, bf16[9,64,8,64]{1,3,2,0:T(8,128)(2,1)S(1)} %copy.42, bf16[9,576,8,64]{1,3,2,0:T(8,128)(2,1)} %copy.48), kind=kOutput, calls=%fused_computation.81 | convolution fusion | flops 350356032 | bytes 17713152 | tf_op jit(solution)/shard_map/sub | solution.py:85
  197.0 10.8 %convolution_bitcast_fusion = f32[9,576,8,64]{1,3,2,0:T(8,128)} fusion(bf16[9,64,8,64]{1,3,2,0:T(8,128)(2,1)} %copy.43, f32[9,8,64,576]{3,2,1,0:T(8,128)} %get-tuple-element.24, f32[9,8,64]{2,1,0:T(8,128)S(1)} %get-tuple-element.23), kind=kOutput, calls=%fused_computation.27 | convolution fusion | flops 345047040 | bytes 21841920 | tf_op jit(solution)/shard_map/bhtk,bthd->bkhd/dot_general | solution.py:100
  207.8 14.6 %fusion.1 = (f32[9,8,64]{2,1,0:T(8,128)S(1)}, f32[9,8,576,64]{2,3,1,0:T(8,128)}) fusion(f32[9,8,64,576]{3,2,1,0:T(8,128)} %get-tuple-element.24, f32[9,8,64]{2,1,0:T(8,128)S(1)} %get-tuple-element.23, bf16[9,64,8,64]{1,3,2,0:T(8,128)(2,1)S(1)} %copy-done.5, bf16[9,576,8,64]{3,2,1,0:T(8,128)(2,1)} %get-tuple-element.3), kind=kOutput, calls=%fused_computation.12 | convolution fusion | flops 353005056 | bytes 27168768 | tf_op jit(solution)/shard_map/bthd,bkhd->bhtk/dot_general | solution.py:88
  222.4 8.9 %fusion.3 = bf16[9,8,64,576]{3,2,1,0:T(8,128)(2,1)S(1)} fusion(f32[9,8,576,64]{2,3,1,0:T(8,128)} %get-tuple-element.26, f32[9,8,64]{2,1,0:T(8,128)S(1)} %get-tuple-element.25, f32[9,8,64,576]{3,2,1,0:T(8,128)} %get-tuple-element.24, f32[9,8,64]{2,1,0:T(8,128)S(1)} %get-tuple-element.23), kind=kLoop, calls=%fused_computation.14 | loop fusion | flops 10616832 | bytes 26578944 | tf_op jit(solution)/shard_map/convert_element_type | solution.py:90
  233.8 13.4 %pad_maximum_fusion = f32[9,576,8,128]{1,3,2,0:T(8,128)} fusion(f32[9,576,8,64]{1,3,2,0:T(8,128)} %convolution_bitcast_fusion, f32[9,576,8,64]{1,3,2,0:T(8,128)S(1)} %multiply_bitcast_fusion), kind=kLoop, calls=%fused_computation.9 | loop fusion | flops 5308416 | bytes 42467328 | tf_op jit(solution)/shard_map/concatenate | solution.py:103
  247.2 23.4 %copy.44 = f32[9,576,8,128]{3,2,1,0:T(8,128)} copy(f32[9,576,8,128]{1,3,2,0:T(8,128)} %pad_maximum_fusion) | data formatting | bytes 42467328 | tf_op jit(solution)/shard_map/concatenate | solution.py:103
  270.6 4.4 broadcast_in_dim.37
  275.0 49.7 %scatter_fusion = f32[33,64,8,128]{3,2,1,0:T(8,128)} fusion(f32[33,64,8,128]{3,2,1,0:T(8,128)} %broadcast_in_dim.37, s32[81]{0:T(128)S(1)} %copy-done.15, f32[81,64,8,128]{3,2,1,0:T(8,128)} %bitcast.124), kind=kCustom, calls=%fused_computation.6 | custom fusion | flops 5308416 | bytes 63701316 | tf_op jit(solution)/shard_map/scatter-add | solution.py:106
  324.7 5.0 %slice.129 = bf16[24,64,8,128]{3,2,1,0:T(8,128)(2,1)} slice(f32[33,64,8,128]{3,2,1,0:T(8,128)} %scatter_fusion), slice={[9:33], [0:64], [0:8], [0:128]} | slice | bytes 6291456 | tf_op jit(solution)/shard_map/slice | solution.py:108
  329.8 15.4 %gather_fusion.5 = bf16[1536,8,128]{2,1,0:T(8,128)(2,1)} fusion(bf16[24,64,8,128]{3,2,1,0:T(8,128)(2,1)} %slice.129, s32[1536]{0:T(1024)S(1)} %reshape.363), kind=kCustom, calls=%fused_computation.5 | custom fusion | bytes 6303744 | tf_op jit(solution)/shard_map/jit(take_along_axis)/gather | solution.py:108
  345.1 5.7 %select_convert_fusion = bf16[24,64,8,128]{3,2,1,0:T(8,128)(2,1)S(1)} fusion(bf16[24,64,8,128]{3,2,1,0:T(8,128)(2,1)} %bitcast.128, pred[24,64]{1,0:T(8,128)(4,1)S(1)} %copy-done.14), kind=kLoop, calls=%fused_computation.21 | loop fusion | flops 1572864 | bytes 6292992 | tf_op jit(solution)/shard_map/convert_element_type | solution.py:109
  354.4 3.2 collective-permute-start.9
  357.7 4.7 %fusion.10 = bf16[9,64,8,64]{1,3,2,0:T(8,128)(2,1)S(1)} fusion(bf16[9,576,8,64]{1,3,2,0:T(8,128)(2,1)} %copy.48, bf16[9,8,64,576]{3,2,1,0:T(8,128)(2,1)S(1)} %bitcast.126), kind=kOutput, calls=%fused_computation.31 | convolution fusion | flops 340328448 | bytes 11206656 | tf_op jit(solution)/shard_map/bhtk,bkhd->bthd/dot_general | solution.py:92
  366.0 2.7 all_to_all.102
  368.8 4.7 %all-to-all-start.4 = ((bf16[4,144,512]{2,1,0:T(8,128)(2,1)}), bf16[4,144,512]{2,1,0:T(8,128)(2,1)S(1)}, u32[]{:S(2)}, u32[]{:S(2)}) async-start(bf16[4,144,512]{2,1,0:T(8,128)(2,1)} %all_to_all.102), calls=%async_computation.4 | async-start | bytes 1179648 | tf_op jit(solution)/shard_map/all_to_all | solution.py:120
  373.5 5.7 %collective-permute-start.10 = (bf16[3,64,8,128]{3,2,1,0:T(8,128)(2,1)}, bf16[3,64,8,128]{3,2,1,0:T(8,128)(2,1)S(1)}, u32[]{:S(2)}, u32[]{:S(2)}) collective-permute-start(bf16[3,64,8,128]{3,2,1,0:T(8,128)(2,1)} %get-tuple-element.10), channel_id=1, source_target_pairs={{4,0},{8,4},{12,8},{16,12},{20,16},{24,20},{28,24},{5,1},{9,5},{13... | collective-permute-start | bytes 1179656 | tf_op jit(solution)/shard_map/ppermute | solution.py:24
  383.5 3.3 collective-permute-start.13
  393.4 3.3 collective-permute-done.13
  396.7 6.3 %collective-permute-done.14 = bf16[3,64,8,128]{3,2,1,0:T(8,128)(2,1)S(1)} collective-permute-done((bf16[3,64,8,128]{3,2,1,0:T(8,128)(2,1)}, bf16[3,64,8,128]{3,2,1,0:T(8,128)(2,1)S(1)}, u32[]{:S(2)}, u32[]{:S(2)}) %collective-permute-start.14) | collective-permute-done | bytes 393248 | tf_op jit(solution)/shard_map/ppermute | solution.py:24
  403.0 9.3 %collective-permute-done.15 = bf16[3,64,8,128]{3,2,1,0:T(8,128)(2,1)S(1)} collective-permute-done((bf16[3,64,8,128]{3,2,1,0:T(8,128)(2,1)S(1)}, bf16[3,64,8,128]{3,2,1,0:T(8,128)(2,1)S(1)}, u32[]{:S(2)}, u32[]{:S(2)}) %collective-permute-start.15) | collective-permute-done | bytes 393248 | tf_op jit(solution)/shard_map/ppermute | solution.py:24
  412.4 3.6 bitcast_convert_fusion
  416.0 9.1 %scatter_fusion.1 = f32[9,64,8,128]{3,2,1,0:T(8,128)S(1)} fusion(f32[9,64,8,128]{3,2,1,0:T(8,128)S(1)} %slice.128, s32[24]{0:T(128)S(1)} %copy-done.16, f32[24,64,8,128]{3,2,1,0:T(8,128)} %bitcast_convert_fusion), kind=kCustom, calls=%fused_computation.7 | custom fusion | flops 1572864 | bytes 18874464 | tf_op jit(solution)/shard_map/scatter-add | solution.py:116
  427.4 4.8 %all-to-all-start.5 = ((bf16[4,144,512]{2,1,0:T(8,128)(2,1)}), bf16[4,144,512]{2,1,0:T(8,128)(2,1)S(1)}, u32[]{:S(2)}, u32[]{:S(2)}) async-start(bf16[4,144,512]{2,1,0:T(8,128)(2,1)} %all_to_all.106), calls=%async_computation.5 | async-start | bytes 1179648 | tf_op jit(solution)/shard_map/all_to_all | solution.py:121
  433.7 12.4 %all-to-all-done.5 = bf16[4,144,512]{2,1,0:T(8,128)(2,1)S(1)} async-done(((bf16[4,144,512]{2,1,0:T(8,128)(2,1)}), bf16[4,144,512]{2,1,0:T(8,128)(2,1)S(1)}, u32[]{:S(2)}, u32[]{:S(2)}) %all-to-all-start.5) | async-done | bytes 589856 | tf_op jit(solution)/shard_map/all_to_all | solution.py:121
  446.1 3.5 all-to-all-start.6
  451.3 12.5 %all-to-all-done.6 = bf16[4,144,512]{2,1,0:T(8,128)(2,1)S(1)} async-done(((bf16[4,144,512]{2,1,0:T(8,128)(2,1)}), bf16[4,144,512]{2,1,0:T(8,128)(2,1)S(1)}, u32[]{:S(2)}, u32[]{:S(2)}) %all-to-all-start.6) | async-done | bytes 589856 | tf_op jit(solution)/shard_map/all_to_all | solution.py:122
  (126 shorter events, 68.5 us)
Async XLA Ops:
  0.6 26.5 %copy-start.10 = (s32[8,64]{1,0:T(8,128)S(1)}, s32[8,64]{1,0:T(8,128)}, u32[]{:S(2)}) copy-start(s32[8,64]{1,0:T(8,128)} %constant.31.clone) | copy-start | bytes 6148
  0.6 26.4 %copy-start.18 = (s32[1,8]{1,0:T(1,128)S(1)}, s32[1,8]{1,0:T(1,128)}, u32[]{:S(2)}) copy-start(s32[1,8]{1,0:T(1,128)} %param.17) | copy-start | bytes 100
  0.7 27.0 %copy-start.6 = (bf16[144,2048]{1,0:T(8,128)(2,1)S(1)}, bf16[144,2048]{1,0:T(8,128)(2,1)}, u32[]{:S(2)}) copy-start(bf16[144,2048]{1,0:T(8,128)(2,1)} %param.10) | copy-start | bytes 1769476
  2.7 43.9 %copy-start.13 = (s32[9,9]{1,0:T(8,128)S(1)}, s32[9,9]{1,0:T(8,128)}, u32[]{:S(2)}) copy-start(s32[9,9]{1,0:T(8,128)} %param.15) | copy-start | bytes 976
  2.7 44.6 %copy-start.17 = (s32[1,8,3]{1,0,2:T(1,128)S(1)}, s32[1,8,3]{1,0,2:T(1,128)}, u32[]{:S(2)}) copy-start(s32[1,8,3]{1,0,2:T(1,128)} %param.16) | copy-start | bytes 292
  2.7 45.3 %copy-start.9 = (s32[8,64]{1,0:T(8,128)S(1)}, s32[8,64]{1,0:T(8,128)}, u32[]{:S(2)}) copy-start(s32[8,64]{1,0:T(8,128)} %constant.32.clone) | copy-start | bytes 6148
  2.7 46.6 %copy-start.7 = (bf16[144,2048]{1,0:T(8,128)(2,1)S(1)}, bf16[144,2048]{1,0:T(8,128)(2,1)}, u32[]{:S(2)}) copy-start(bf16[144,2048]{1,0:T(8,128)(2,1)} %param.13) | copy-start | bytes 1769476
  2.7 20.9 %all-to-all-start.1 = ((bf16[144,4,512]{2,0,1:T(8,128)(2,1)}), bf16[144,4,512]{2,0,1:T(8,128)(2,1)S(1)}, u32[]{:S(2)}, u32[]{:S(2)}) async-start(bf16[144,4,512]{2,0,1:T(8,128)(2,1)} %bitcast.121), calls=%async_computation.1 | async-start | bytes 1179648 | tf_op jit(solution)/shard_map/all_to_all | solution.py:53
  23.6 18.9 %all-to-all-start = ((bf16[144,4,512]{2,0,1:T(8,128)(2,1)}), bf16[144,4,512]{2,0,1:T(8,128)(2,1)S(1)}, u32[]{:S(2)}, u32[]{:S(2)}) async-start(bf16[144,4,512]{2,0,1:T(8,128)(2,1)} %bitcast.122), calls=%async_computation | async-start | bytes 1179648 | tf_op jit(solution)/shard_map/all_to_all | solution.py:52
  42.4 9.0 %copy-start.3 = (bf16[144,4,512]{2,0,1:T(8,128)(2,1)}, bf16[144,4,512]{2,0,1:T(8,128)(2,1)S(1)}, u32[]{:S(2)}) copy-start(bf16[144,4,512]{2,0,1:T(8,128)(2,1)S(1)} %all-to-all-done) | copy-start | bytes 1769476
  42.4 18.8 %all-to-all-start.2 = ((bf16[144,4,512]{2,0,1:T(8,128)(2,1)}), bf16[144,4,512]{2,0,1:T(8,128)(2,1)S(1)}, u32[]{:S(2)}, u32[]{:S(2)}) async-start(bf16[144,4,512]{2,0,1:T(8,128)(2,1)} %bitcast.120), calls=%async_computation.2 | async-start | bytes 1179648 | tf_op jit(solution)/shard_map/all_to_all | solution.py:51
  61.3 0.8 copy-start.1
  62.1 29.2 %all-to-all-start.3 = ((bf16[144,4,512]{2,0,1:T(8,128)(2,1)}), bf16[144,4,512]{2,0,1:T(8,128)(2,1)}, u32[]{:S(2)}, u32[]{:S(2)}) async-start(bf16[144,4,512]{2,0,1:T(8,128)(2,1)} %bitcast.133), calls=%async_computation.3 | async-start | bytes 1179648 | tf_op jit(solution)/shard_map/all_to_all | solution.py:54
  69.7 5.6 %copy-start.11 = (s32[24,64]{1,0:T(8,128)S(1)}, s32[24,64]{1,0:T(8,128)}, u32[]{:S(2)}) copy-start(s32[24,64]{1,0:T(8,128)} %broadcast_in_dim_reshape.11) | copy-start | bytes 18436
  69.7 8.9 %copy-start.12 = (s32[24,64]{1,0:T(8,128)S(1)}, s32[24,64]{1,0:T(8,128)}, u32[]{:S(2)}) copy-start(s32[24,64]{1,0:T(8,128)} %broadcast_in_dim_reshape.13) | copy-start | bytes 18436
  69.7 17.9 %copy-start.2 = (bf16[144,4,512]{2,0,1:T(8,128)(2,1)S(1)}, bf16[144,4,512]{2,0,1:T(8,128)(2,1)}, u32[]{:S(2)}) copy-start(bf16[144,4,512]{2,0,1:T(8,128)(2,1)} %copy-done.1) | copy-start | bytes 1769476
  73.3 26.9 %collective-permute-start = (bf16[3,64,8,128]{3,2,1,0:T(8,128)(2,1)}, bf16[3,64,8,128]{3,2,1,0:T(8,128)(2,1)}, u32[]{:S(2)}, u32[]{:S(2)}) collective-permute-start(bf16[3,64,8,128]{3,2,1,0:T(8,128)(2,1)} %get-tuple-element.20), channel_id=1, source_target_pairs={{0,12},{4,16},{8,20},{12,24},{16,28},{1,13},{5,17},{9,21},{13,25},... | collective-permute-start | bytes 1179656 | tf_op jit(solution)/shard_map/ppermute | solution.py:24
  75.9 28.0 %collective-permute-start.1 = (bf16[3,64,8,128]{3,2,1,0:T(8,128)(2,1)}, bf16[3,64,8,128]{3,2,1,0:T(8,128)(2,1)}, u32[]{:S(2)}, u32[]{:S(2)}) collective-permute-start(bf16[3,64,8,128]{3,2,1,0:T(8,128)(2,1)} %get-tuple-element.19), channel_id=1, source_target_pairs={{0,8},{4,12},{8,16},{12,20},{16,24},{20,28},{1,9},{5,13},{9,17},{1... | collective-permute-start | bytes 1179656 | tf_op jit(solution)/shard_map/ppermute | solution.py:24
  79.2 29.0 %collective-permute-start.2 = (bf16[3,64,8,128]{3,2,1,0:T(8,128)(2,1)}, bf16[3,64,8,128]{3,2,1,0:T(8,128)(2,1)}, u32[]{:S(2)}, u32[]{:S(2)}) collective-permute-start(bf16[3,64,8,128]{3,2,1,0:T(8,128)(2,1)} %get-tuple-element.18), channel_id=1, source_target_pairs={{0,4},{4,8},{8,12},{12,16},{16,20},{20,24},{24,28},{1,5},{5,9},{9,... | collective-permute-start | bytes 1179656 | tf_op jit(solution)/shard_map/ppermute | solution.py:24
  81.1 30.9 %collective-permute-start.3 = (bf16[3,64,8,128]{3,2,1,0:T(8,128)(2,1)}, bf16[3,64,8,128]{3,2,1,0:T(8,128)(2,1)}, u32[]{:S(2)}, u32[]{:S(2)}) collective-permute-start(bf16[3,64,8,128]{3,2,1,0:T(8,128)(2,1)} %get-tuple-element.17), channel_id=1, source_target_pairs={{0,4},{4,8},{8,12},{12,16},{16,20},{20,24},{24,28},{1,5},{5,9},{9,... | collective-permute-start | bytes 1179656 | tf_op jit(solution)/shard_map/ppermute | solution.py:24
  83.0 30.8 %collective-permute-start.4 = (bf16[3,64,8,128]{3,2,1,0:T(8,128)(2,1)}, bf16[3,64,8,128]{3,2,1,0:T(8,128)(2,1)}, u32[]{:S(2)}, u32[]{:S(2)}) collective-permute-start(bf16[3,64,8,128]{3,2,1,0:T(8,128)(2,1)} %get-tuple-element.16), channel_id=1, source_target_pairs={{4,0},{8,4},{12,8},{16,12},{20,16},{24,20},{28,24},{5,1},{9,5},{13... | collective-permute-start | bytes 1179656 | tf_op jit(solution)/shard_map/ppermute | solution.py:24
  100.2 15.4 %collective-permute-start.5 = (bf16[3,64,8,128]{3,2,1,0:T(8,128)(2,1)}, bf16[3,64,8,128]{3,2,1,0:T(8,128)(2,1)S(1)}, u32[]{:S(2)}, u32[]{:S(2)}) collective-permute-start(bf16[3,64,8,128]{3,2,1,0:T(8,128)(2,1)} %get-tuple-element.15), channel_id=1, source_target_pairs={{4,0},{8,4},{12,8},{16,12},{20,16},{24,20},{28,24},{5,1},{9,5},{13... | collective-permute-start | bytes 1179656 | tf_op jit(solution)/shard_map/ppermute | solution.py:24
  103.9 14.0 %collective-permute-start.6 = (bf16[3,64,8,128]{3,2,1,0:T(8,128)(2,1)}, bf16[3,64,8,128]{3,2,1,0:T(8,128)(2,1)S(1)}, u32[]{:S(2)}, u32[]{:S(2)}) collective-permute-start(bf16[3,64,8,128]{3,2,1,0:T(8,128)(2,1)} %get-tuple-element.14), channel_id=1, source_target_pairs={{8,0},{12,4},{16,8},{20,12},{24,16},{28,20},{9,1},{13,5},{17,9},{2... | collective-permute-start | bytes 1179656 | tf_op jit(solution)/shard_map/ppermute | solution.py:24
  108.2 13.6 %collective-permute-start.7 = (bf16[3,64,8,128]{3,2,1,0:T(8,128)(2,1)}, bf16[3,64,8,128]{3,2,1,0:T(8,128)(2,1)S(1)}, u32[]{:S(2)}, u32[]{:S(2)}) collective-permute-start(bf16[3,64,8,128]{3,2,1,0:T(8,128)(2,1)} %get-tuple-element.13), channel_id=1, source_target_pairs={{12,0},{16,4},{20,8},{24,12},{28,16},{13,1},{17,5},{21,9},{25,13},... | collective-permute-start | bytes 1179656 | tf_op jit(solution)/shard_map/ppermute | solution.py:24
  171.9 14.1 %copy-start.4 = (f32[8,64,576]{2,1,0:T(8,128)S(1)}, f32[8,64,576]{2,1,0:T(8,128)}, u32[]{:S(2)}) copy-start(f32[8,64,576]{2,1,0:T(8,128)} %param.14) | copy-start | bytes 3538948
  197.0 10.8 %copy-start.5 = (bf16[9,64,8,64]{1,3,2,0:T(8,128)(2,1)S(1)}, bf16[9,64,8,64]{1,3,2,0:T(8,128)(2,1)}, u32[]{:S(2)}) copy-start(bf16[9,64,8,64]{1,3,2,0:T(8,128)(2,1)} %copy.43) | copy-start | bytes 1769476
  231.4 2.5 copy-start
  270.6 4.4 copy-start.15
  329.7 15.4 %copy-start.14 = (pred[24,64]{1,0:T(8,128)(4,1)S(1)}, pred[24,64]{1,0:T(8,128)(4,1)}, u32[]{:S(2)}) copy-start(pred[24,64]{1,0:T(8,128)(4,1)} %compare_and_fusion) | copy-start | bytes 4612
  329.7 27.9 %slice-start = ((s8[5898240]{0:T(1024)(128)(4,1)}), s8[1703936]{0:T(1024)(128)(4,1)S(1)}, s32[]{:S(2)}) async-start(s8[5898240]{0:T(1024)(128)(4,1)} %bitcast.125), calls=%async_computation.7 | async-start | bytes 3407872
  345.1 12.6 %slice-start.1 = ((s8[5898240]{0:T(1024)(128)(4,1)}), s8[4194304]{0:T(1024)(128)(4,1)S(1)}, s32[]{:S(2)}) async-start(s8[5898240]{0:T(1024)(128)(4,1)} %bitcast.125), calls=%async_computation.8 | async-start | bytes 8388608
  352.5 31.0 %collective-permute-start.8 = (bf16[3,64,8,128]{3,2,1,0:T(8,128)(2,1)}, bf16[3,64,8,128]{3,2,1,0:T(8,128)(2,1)}, u32[]{:S(2)}, u32[]{:S(2)}) collective-permute-start(bf16[3,64,8,128]{3,2,1,0:T(8,128)(2,1)} %get-tuple-element.12), channel_id=1, source_target_pairs={{12,0},{16,4},{20,8},{24,12},{28,16},{13,1},{17,5},{21,9},{25,13},... | collective-permute-start | bytes 1179656 | tf_op jit(solution)/shard_map/ppermute | solution.py:24
  354.4 33.4 %collective-permute-start.9 = (bf16[3,64,8,128]{3,2,1,0:T(8,128)(2,1)}, bf16[3,64,8,128]{3,2,1,0:T(8,128)(2,1)}, u32[]{:S(2)}, u32[]{:S(2)}) collective-permute-start(bf16[3,64,8,128]{3,2,1,0:T(8,128)(2,1)} %get-tuple-element.11), channel_id=1, source_target_pairs={{8,0},{12,4},{16,8},{20,12},{24,16},{28,20},{9,1},{13,5},{17,9},{2... | collective-permute-start | bytes 1179656 | tf_op jit(solution)/shard_map/ppermute | solution.py:24
  366.0 25.2 %copy-start.8 = (bf16[3,64,8,128]{3,2,1,0:T(8,128)(2,1)S(1)}, bf16[3,64,8,128]{3,2,1,0:T(8,128)(2,1)}, u32[]{:S(2)}) copy-start(bf16[3,64,8,128]{3,2,1,0:T(8,128)(2,1)} %get-tuple-element.5) | copy-start | bytes 1179652
  368.8 58.6 %all-to-all-start.4 = ((bf16[4,144,512]{2,1,0:T(8,128)(2,1)}), bf16[4,144,512]{2,1,0:T(8,128)(2,1)S(1)}, u32[]{:S(2)}, u32[]{:S(2)}) async-start(bf16[4,144,512]{2,1,0:T(8,128)(2,1)} %all_to_all.102), calls=%async_computation.4 | async-start | bytes 1179648 | tf_op jit(solution)/shard_map/all_to_all | solution.py:120
  373.5 17.7 %collective-permute-start.10 = (bf16[3,64,8,128]{3,2,1,0:T(8,128)(2,1)}, bf16[3,64,8,128]{3,2,1,0:T(8,128)(2,1)S(1)}, u32[]{:S(2)}, u32[]{:S(2)}) collective-permute-start(bf16[3,64,8,128]{3,2,1,0:T(8,128)(2,1)} %get-tuple-element.10), channel_id=1, source_target_pairs={{4,0},{8,4},{12,8},{16,12},{20,16},{24,20},{28,24},{5,1},{9,5},{13... | collective-permute-start | bytes 1179656 | tf_op jit(solution)/shard_map/ppermute | solution.py:24
  379.2 14.0 %collective-permute-start.11 = (bf16[3,64,8,128]{3,2,1,0:T(8,128)(2,1)}, bf16[3,64,8,128]{3,2,1,0:T(8,128)(2,1)S(1)}, u32[]{:S(2)}, u32[]{:S(2)}) collective-permute-start(bf16[3,64,8,128]{3,2,1,0:T(8,128)(2,1)} %get-tuple-element.9), channel_id=1, source_target_pairs={{4,0},{8,4},{12,8},{16,12},{20,16},{24,20},{28,24},{5,1},{9,5},{13... | collective-permute-start | bytes 1179656 | tf_op jit(solution)/shard_map/ppermute | solution.py:24
  381.1 12.2 %collective-permute-start.12 = (bf16[3,64,8,128]{3,2,1,0:T(8,128)(2,1)}, bf16[3,64,8,128]{3,2,1,0:T(8,128)(2,1)S(1)}, u32[]{:S(2)}, u32[]{:S(2)}) collective-permute-start(bf16[3,64,8,128]{3,2,1,0:T(8,128)(2,1)} %get-tuple-element.8), channel_id=1, source_target_pairs={{0,4},{4,8},{8,12},{12,16},{16,20},{20,24},{24,28},{1,5},{5,9},{9,... | collective-permute-start | bytes 1179656 | tf_op jit(solution)/shard_map/ppermute | solution.py:24
  383.5 13.1 %collective-permute-start.13 = (bf16[3,64,8,128]{3,2,1,0:T(8,128)(2,1)}, bf16[3,64,8,128]{3,2,1,0:T(8,128)(2,1)S(1)}, u32[]{:S(2)}, u32[]{:S(2)}) collective-permute-start(bf16[3,64,8,128]{3,2,1,0:T(8,128)(2,1)} %get-tuple-element.7), channel_id=1, source_target_pairs={{0,4},{4,8},{8,12},{12,16},{16,20},{20,24},{24,28},{1,5},{5,9},{9,... | collective-permute-start | bytes 1179656 | tf_op jit(solution)/shard_map/ppermute | solution.py:24
  387.8 15.2 %collective-permute-start.14 = (bf16[3,64,8,128]{3,2,1,0:T(8,128)(2,1)}, bf16[3,64,8,128]{3,2,1,0:T(8,128)(2,1)S(1)}, u32[]{:S(2)}, u32[]{:S(2)}) collective-permute-start(bf16[3,64,8,128]{3,2,1,0:T(8,128)(2,1)} %get-tuple-element.6), channel_id=1, source_target_pairs={{0,8},{4,12},{8,16},{12,20},{16,24},{20,28},{1,9},{5,13},{9,17},{1... | collective-permute-start | bytes 1179656 | tf_op jit(solution)/shard_map/ppermute | solution.py:24
  391.2 21.1 %collective-permute-start.15 = (bf16[3,64,8,128]{3,2,1,0:T(8,128)(2,1)S(1)}, bf16[3,64,8,128]{3,2,1,0:T(8,128)(2,1)S(1)}, u32[]{:S(2)}, u32[]{:S(2)}) collective-permute-start(bf16[3,64,8,128]{3,2,1,0:T(8,128)(2,1)S(1)} %copy-done.8), channel_id=1, source_target_pairs={{0,12},{4,16},{8,20},{12,24},{16,28},{1,13},{5,17},{9,21},{13,25},... | collective-permute-start | bytes 1179656 | tf_op jit(solution)/shard_map/ppermute | solution.py:24
  412.4 3.6 copy-start.16
  427.4 18.7 %all-to-all-start.5 = ((bf16[4,144,512]{2,1,0:T(8,128)(2,1)}), bf16[4,144,512]{2,1,0:T(8,128)(2,1)S(1)}, u32[]{:S(2)}, u32[]{:S(2)}) async-start(bf16[4,144,512]{2,1,0:T(8,128)(2,1)} %all_to_all.106), calls=%async_computation.5 | async-start | bytes 1179648 | tf_op jit(solution)/shard_map/all_to_all | solution.py:121
  446.1 17.7 %all-to-all-start.6 = ((bf16[4,144,512]{2,1,0:T(8,128)(2,1)}), bf16[4,144,512]{2,1,0:T(8,128)(2,1)S(1)}, u32[]{:S(2)}, u32[]{:S(2)}) async-start(bf16[4,144,512]{2,1,0:T(8,128)(2,1)} %all_to_all.110), calls=%async_computation.6 | async-start | bytes 1179648 | tf_op jit(solution)/shard_map/all_to_all | solution.py:122
where the time goes:
time: 467 us; the launch traced here: 465 us
  local copies, waits for them, and re-layouts  160 us (34%)
  other arithmetic  101 us (22%)
  waiting for transfers between devices  88.2 us (19%)
  starting transfers between devices  71.3 us (15%)
  matrix products  42.9 us (9%)
    scatter-add x1, other arithmetic, per_device(): jax.ops.segment_sum(window_grad, near_ids, num_segments=slot_total)  49.7 us
    ppermute x16, starting transfers between devices, from_behind(): lax.ppermute(value, axis, [(source, source + steps) for source in range(f...  42.2 us
    unnamed x58, local copies, waits for them, and re-layouts  28.5 us
    ppermute x16, waiting for transfers between devices, from_behind(): lax.ppermute(value, axis, [(source, source + steps) for source in range(f...  27.4 us
    concatenate x1, local copies, waits for them, and re-layouts, per_device(): jnp.concatenate([grad_kw, grad_vw], axis=-1)  23.4 us
    slice x1, local copies, waits for them, and re-layouts, per_device(): win_v = window[..., HD:]  17.1 us
    gather x2, local copies, waits for them, and re-layouts, per_device(): jnp.take_along_axis(slot_grad[QB_DOM:], back_order[:, :, None, None], axi...  15.5 us
    gather x2, local copies, waits for them, and re-layouts, per_device(): jnp.take_along_axis(arrived, turn_index[:, :, None, None], axis=1)  15.3 us
  transfers between devices with their start and end apart: 23, of which 11 were waited for; matrix products, arithmetic and copies ran while one was open for 14% of the time, Pallas kernels for 0%

commit v1 on v0

v1 whole, which is shorter than its diff:
```python
import functools

import jax
import jax.numpy as jnp
import numpy as np
from jax import lax
from jax.experimental import pallas as pl
from jax.experimental.pallas import tpu as pltpu
from jax.sharding import PartitionSpec as P

HD = 64
PATCH = 8
BT = 64
GRID_ROWS = 4
DIRS = 8
WIN = 9
WINK = 576
QB_DOM = 9
CAP = 3
GROUP_HEADS = 4
VMEM_LIMIT = 48 * 1024 * 1024

OFFSET_LIST = [(-1, -1), (-1, 0), (-1, 1), (0, -1), (0, 1), (1, -1), (1, 0), (1, 1)]


class Plan:
    def __init__(self, domains):
        grid_cols = domains // GRID_ROWS
        groups = []
        for k, (row_step, col_step) in enumerate(OFFSET_LIST):
            pairs = []
            for d in range(domains):
                row, col = d // grid_cols + row_step, d % grid_cols + col_step
                if 0 <= row < GRID_ROWS and 0 <= col < grid_cols:
                    pairs.append((row * grid_cols + col, d))
            count = 1 if row_step and col_step else CAP
            if not pairs:
                continue
            lenders, borrowers = {p for p, _ in pairs}, {d for _, d in pairs}
            for group in groups:
                taken_l = {p for p, _ in group["pairs"]}
                taken_b = {d for _, d in group["pairs"]}
                if group["count"] == count and not (taken_l & lenders) and not (taken_b & borrowers):
                    break
            else:
                group = dict(count=count, pairs=[], send=[0] * domains, recv=[0] * domains)
                groups.append(group)
            group["pairs"] += pairs
            for p, d in pairs:
                group["send"][p] = k
                group["recv"][d] = k
        groups.sort(key=lambda group: -group["count"])
        self.groups = groups
        self.counts = [group["count"] for group in groups]
        self.offsets = [sum(self.counts[:i]) for i in range(len(groups))]
        self.borrowed = sum(self.counts)
        self.slots = QB_DOM + self.borrowed
        slot_total = QB_DOM + DIRS * CAP
        table = np.zeros((domains, slot_total + 2 * len(groups)), np.int32)
        for d in range(domains):
            table[d, :QB_DOM] = np.arange(QB_DOM)
            for i, group in enumerate(groups):
                k = group["recv"][d]
                for c in range(CAP if any(d == to for _, to in group["pairs"]) else 0):
                    place = QB_DOM + self.offsets[i] + (c if group["count"] > 1 else 0)
                    table[d, QB_DOM + k * CAP + c] = place
                table[d, slot_total + i] = group["send"][d]
                table[d, slot_total + len(groups) + i] = k
        self.table = table
        self.send_at = slot_total
        self.recv_at = slot_total + len(groups)

    def lent_block(self, i, c, table_ref, send_ref):
        k = table_ref[self.send_at + i]
        if self.counts[i] > 1:
            return send_ref[k * CAP + c]
        found = send_ref[k * CAP]
        for other in range(1, CAP):
            found = jnp.maximum(found, send_ref[k * CAP + other])
        return found


def block_rows(index):
    return pl.ds(pl.multiple_of(index * BT, BT), BT)


def turn_matrix(orient, back):
    token = lax.broadcasted_iota(jnp.int32, (BT, BT), 1 if back else 0)
    place = lax.broadcasted_iota(jnp.int32, (BT, BT), 0 if back else 1)
    row, col = token >> 3, token & (PATCH - 1)
    row = jnp.where((orient & 1) == 1, PATCH - 1 - row, row)
    col = jnp.where(((orient >> 1) & 1) == 1, PATCH - 1 - col, col)
    mapped = jnp.where(orient >= 4, PATCH * col + row, PATCH * row + col)
    return (mapped == place).astype(jnp.float32).astype(jnp.bfloat16)


def lend_kernel(plan, table_ref, send_ref, kv_ref, *out_refs):
    for i, count in enumerate(plan.counts):
        for c in range(count):
            block = plan.lent_block(i, c, table_ref, send_ref)
            out_refs[i][c * BT:(c + 1) * BT, :] = kv_ref[block_rows(block), :]


def settle_kernel(plan, table_ref, send_ref, own_ref, *refs):
    out_ref, total = refs[-2:]
    total[...] = own_ref[...]
    for i, count in enumerate(plan.counts):
        for c in range(count):
            block = plan.lent_block(i, c, table_ref, send_ref)
            total[block_rows(block), :] += refs[i][c * BT:(c + 1) * BT, :].astype(jnp.float32)
    out_ref[...] = total[...].astype(jnp.bfloat16)


def dot(a, b, contract):
    return lax.dot_general(a, b, ((contract[:1], contract[1:]), ((), ())),
                           preferred_element_type=jnp.float32)


def attend_kernel(plan, heads, table_ref, near_ref, orient_ref, qg_ref, kv_ref, bias_ref, *refs):
    groups = len(plan.groups)
    arrived = refs[:groups]
    dq_ref, own_ref = refs[groups:groups + 2]
    leaving = refs[groups + 2:2 * groups + 2]
    ext, acc, win = refs[2 * groups + 2:]
    width = heads * HD
    some = min(heads, GROUP_HEADS)
    lanes = some * HD
    scale = HD ** -0.5

    ext[:QB_DOM * BT, :] = kv_ref[...]
    for i, count in enumerate(plan.counts):
        turn = turn_matrix(orient_ref[table_ref[plan.recv_at + i]], False)
        for c in range(count):
            at = (QB_DOM + plan.offsets[i] + c) * BT
            ext[at:at + BT, :] = dot(turn, arrived[i][c * BT:(c + 1) * BT, :], (1, 0)).astype(jnp.bfloat16)
    acc[...] = jnp.zeros_like(acc)

    same_head = (lax.broadcasted_iota(jnp.int32, (lanes, lanes), 0) // HD
                 == lax.broadcasted_iota(jnp.int32, (lanes, lanes), 1) // HD)

    def spread(block):
        wide = jnp.concatenate([block] * some, axis=0)
        return jnp.where(same_head, wide, jnp.zeros_like(wide))

    def one_block(b, carry):
        rows = block_rows(b)
        places = [table_ref[near_ref[b * WIN + j]] for j in range(WIN)]
        for j in range(WIN):
            win[j * BT:(j + 1) * BT, :] = ext[block_rows(places[j]), :]
        for part in range(heads // some):
            here = slice(part * lanes, (part + 1) * lanes)
            there = slice(width + part * lanes, width + (part + 1) * lanes)
            win_k, win_v = win[:, here], win[:, there]
            query = spread(qg_ref[rows, here] * jnp.bfloat16(scale))
            grad = spread(qg_ref[rows, there])
            scores = dot(win_k, query, (1, 1)) + bias_ref[:, here]
            weight = jnp.exp(scores - jnp.max(scores, axis=0, keepdims=True))
            probs = weight * (1.0 / jnp.sum(weight, axis=0, keepdims=True))
            probs_half = probs.astype(jnp.bfloat16)
            dprobs = dot(win_v, grad, (1, 1))
            delta = jnp.sum(probs_half.astype(jnp.float32) * dprobs, axis=0, keepdims=True)
            dscores = (probs * (dprobs - delta)).astype(jnp.bfloat16)
            grad_q = dot(dscores, win_k, (0, 0))
            grad_q = jnp.where(same_head, grad_q, 0.0)
            total_q = grad_q[:BT]
            for h in range(1, some):
                total_q = total_q + grad_q[h * BT:(h + 1) * BT]
            dq_ref[rows, here] = (total_q * scale).astype(jnp.bfloat16)
            grad_k = dot(dscores, query, (1, 0))
            grad_v = dot(probs_half, grad, (1, 0))
            for j in range(WIN):
                acc[block_rows(places[j]), here] += grad_k[j * BT:(j + 1) * BT]
                acc[block_rows(places[j]), there] += grad_v[j * BT:(j + 1) * BT]
        return carry

    lax.fori_loop(0, QB_DOM, one_block, 0)
    own_ref[...] = acc[:QB_DOM * BT, :]
    for i, count in enumerate(plan.counts):
        turn = turn_matrix(orient_ref[table_ref[plan.recv_at + i]], True)
        for c in range(count):
            at = (QB_DOM + plan.offsets[i] + c) * BT
            slot = acc[at:at + BT, :].astype(jnp.bfloat16)
            leaving[i][c * BT:(c + 1) * BT, :] = dot(turn, slot, (1, 0)).astype(jnp.bfloat16)


def smem_specs(count):
    return [pl.BlockSpec(memory_space=pltpu.SMEM)] * count


def vmem_specs(count):
    return [pl.BlockSpec(memory_space=pltpu.VMEM)] * count


def params():
    return pltpu.CompilerParams(vmem_limit_bytes=VMEM_LIMIT)


def bf16(*shape):
    return jax.ShapeDtypeStruct(shape, jnp.bfloat16)


def per_device(plan, queries, keys_in, values_in, grad_out, pos_bias, neighbours, send_block, orient):
    heads = pos_bias.shape[0]
    width = heads * HD
    tokens = queries.shape[0]
    holders = lax.axis_size("head")
    tokens_dom = tokens * holders
    groups = len(plan.groups)
    table = lax.dynamic_index_in_dim(jnp.asarray(plan.table), lax.axis_index("dom"), 0, False)
    near, sends, turns = neighbours.reshape(-1), send_block.reshape(-1), orient.reshape(-1)

    def gather_heads(left, right):
        pair = jnp.concatenate([left.reshape(tokens, holders, width), right.reshape(tokens, holders, width)], axis=-1)
        pair = jnp.transpose(pair, (1, 0, 2))
        pair = lax.all_to_all(pair, "head", split_axis=0, concat_axis=0, tiled=True)
        return pair.reshape(tokens_dom, 2 * width)

    def scatter_heads(matrix):
        matrix = matrix.reshape(holders, tokens, matrix.shape[1])
        return lax.all_to_all(matrix, "head", split_axis=0, concat_axis=0, tiled=True)

    def by_token(matrix):
        return jnp.transpose(matrix, (1, 0, 2)).reshape(tokens, holders * width)

    kv = gather_heads(keys_in, values_in)
    qg = gather_heads(queries, grad_out)
    bias = jnp.transpose(pos_bias, (2, 0, 1)).reshape(WINK, heads * BT)

    block_shapes = [bf16(count * BT, 2 * width) for count in plan.counts]
    lent = pl.pallas_call(
        functools.partial(lend_kernel, plan),
        out_shape=block_shapes,
        in_specs=smem_specs(2) + vmem_specs(1),
        out_specs=vmem_specs(groups),
        compiler_params=params(),
        name="lend",
    )(table, sends, kv)
    arrived = [lax.ppermute(lent[i], "dom", group["pairs"]) for i, group in enumerate(plan.groups)]

    outs = pl.pallas_call(
        functools.partial(attend_kernel, plan, heads),
        out_shape=[bf16(tokens_dom, width), jax.ShapeDtypeStruct((tokens_dom, 2 * width), jnp.float32)] + block_shapes,
        in_specs=smem_specs(3) + vmem_specs(3 + groups),
        out_specs=vmem_specs(2 + groups),
        scratch_shapes=[
            pltpu.VMEM((plan.slots * BT, 2 * width), jnp.bfloat16),
            pltpu.VMEM((plan.slots * BT, 2 * width), jnp.float32),
            pltpu.VMEM((WINK, 2 * width), jnp.bfloat16),
        ],
        compiler_params=params(),
        cost_estimate=pl.CostEstimate(flops=5 * 2 * tokens_dom * WINK * width, bytes_accessed=8 * tokens_dom * width,
                                      transcendentals=tokens_dom * WINK * heads),
        name="attend",
    )(table, near, turns, qg, kv, bias, *arrived)
    grad_q, own, leaving = outs[0], outs[1], outs[2:]

    returned = [lax.ppermute(leaving[i], "dom", [(d, p) for p, d in group["pairs"]])
                for i, group in enumerate(plan.groups)]
    grad_q = scatter_heads(grad_q)
    grad_kv = pl.pallas_call(
        functools.partial(settle_kernel, plan),
        out_shape=bf16(tokens_dom, 2 * width),
        in_specs=smem_specs(2) + vmem_specs(1 + groups),
        out_specs=vmem_specs(1)[0],
        scratch_shapes=[pltpu.VMEM((tokens_dom, 2 * width), jnp.float32)],
        compiler_params=params(),
        name="settle",
    )(table, sends, own, *returned)
    grad_kv = scatter_heads(grad_kv)
    return by_token(grad_q), by_token(grad_kv[..., :width]), by_token(grad_kv[..., width:])


def solution(mesh):
    plan = Plan(mesh.shape["dom"])
    tokens = P(("dom", "head"), None)
    return jax.shard_map(
        functools.partial(per_device, plan),
        mesh=mesh,
        in_specs=(
            tokens,
            tokens,
            tokens,
            tokens,
            P("head", None, None),
            P("dom", None),
            P("dom", None, None),
            P("dom", None),
        ),
        out_specs=(tokens, tokens, tokens),
        check_vma=False,
    )
```

time: 467 us -> 168 us (0.36)
  local copies, waits for them, and re-layouts: 160 us -> 14.8 us
  other arithmetic: 101 us -> 2.35 us
  matrix products: 42.9 us -> 0 us
  starting transfers between devices: 71.3 us -> 44.3 us
  Pallas kernels: 0 us -> 25.8 us
  waiting for transfers between devices: 88.2 us -> 78.2 us
    scatter-add x2 -> x0, other arithmetic: 58.9 us -> none  [the longest x1 49.7 us: per_device(): jax.ops.segment_sum(window_grad, near_ids, num_segments=slot_total)]
    gather x8 -> x0, local copies, waits for them, and re-layouts: 43.4 us -> none  [the longest x2 15.5 us: per_device(): jnp.take_along_axis(slot_grad[QB_DOM:], back_order[:, :, None, None], axi...]
    dot_general x4 -> x0, matrix products: 31.8 us -> none  [the longest x1 14.6 us: per_device(): jnp.einsum('bthd,bkhd->bhtk', grad_blk, win_v, preferred_element_type=jnp...]
    slice x6 -> x0, local copies, waits for them, and re-layouts: 29.7 us -> none  [the longest x1 17.1 us: per_device(): win_v = window[..., HD:]]
    pallas_call x0 -> x3, Pallas kernels: none -> 25.8 us  [the longest x1 22 us: per_device(): pl.pallas_call(functools.partial(attend_kernel, plan, heads), out_shape=[...]
    concatenate x1 -> x0, local copies, waits for them, and re-layouts: 23.4 us -> none  [per_device(): jnp.concatenate([grad_kw, grad_vw], axis=-1)]
    unnamed x58 -> x32, local copies, waits for them, and re-layouts: 28.5 us -> 6.4 us
    convert_element_type x3 -> x0, other arithmetic: 18.2 us -> none  [the longest x1 8.94 us: per_device(): dscores = (probs * (dprobs - row_delta)).astype(jnp.bfloat16)]
  transfers between devices with their start and end apart: 23 -> 14, of which waited for: 11 -> 5; matrix products, arithmetic and copies ran while one was open for 14% -> 4% of each run, Pallas kernels for 0% -> 2%
where the time goes in v1:
time: 168 us; the launch traced here: 166 us
  waiting for transfers between devices  78.2 us (47%)
  starting transfers between devices  44.3 us (26%)
  Pallas kernels  25.8 us (15%)
  local copies, waits for them, and re-layouts  14.8 us (9%)
  other arithmetic  2.35 us (1%)
    all_to_all x2, waiting for transfers between devices, gather_heads(): pair = lax.all_to_all(pair, 'head', split_axis=0, concat_axis=0, tiled=True)  35.8 us
    all_to_all x2, waiting for transfers between devices, scatter_heads(): lax.all_to_all(matrix, 'head', split_axis=0, concat_axis=0, tiled=True)  27.5 us
    pallas_call x1, Pallas kernels, per_device(): pl.pallas_call(functools.partial(attend_kernel, plan, heads), out_shape=[...  22 us
    ppermute x5, waiting for transfers between devices, per_device(): lax.ppermute(leaving[i], 'dom', [(d, p) for p, d in group['pairs']])  14.9 us
    ppermute x5, starting transfers between devices, per_device(): lax.ppermute(lent[i], 'dom', group['pairs'])  13.3 us
    ppermute x5, starting transfers between devices, per_device(): lax.ppermute(leaving[i], 'dom', [(d, p) for p, d in group['pairs']])  12.6 us
    all_to_all x2, starting transfers between devices, scatter_heads(): lax.all_to_all(matrix, 'head', split_axis=0, concat_axis=0, tiled=True)  9.92 us
    all_to_all x2, starting transfers between devices, gather_heads(): pair = lax.all_to_all(pair, 'head', split_axis=0, concat_axis=0, tiled=True)  8.53 us
  transfers between devices with their start and end apart: 14, of which 5 were waited for; matrix products, arithmetic and copies ran while one was open for 4% of the time, Pallas kernels for 2%

profile of v1, /device:TPU:4, one launch (start us, length us, event | category | flops | bytes accessed | tf_op | source)
XLA Modules:
  0.0 166.2 jit_solution(2554762007589029440)
XLA Ops:
  0.6 1.3 copy_bitcast_fusion
  2.0 1.2 maximum_bitcast_fusion.1
  3.1 5.0 %all-to-all-start.1 = ((bf16[4,144,1024]{2,1,0:T(8,128)(2,1)}), bf16[4,144,1024]{2,1,0:T(8,128)(2,1)S(1)}, u32[]{:S(2)}, u32[]{:S(2)}) async-start(bf16[4,144,1024]{2,1,0:T(8,128)(2,1)} %maximum_bitcast_fusion.1), calls=%async_computation.1 | async-start | bytes 2359296 | tf_op jit(solution)/shard_map/all_to_all | solution.py:215
  8.1 0.1 copy_bitcast_fusion.2
  8.2 1.2 maximum_bitcast_fusion
  9.4 27.2 %all-to-all-done.1 = bf16[4,144,1024]{2,1,0:T(8,128)(2,1)S(1)} async-done(((bf16[4,144,1024]{2,1,0:T(8,128)(2,1)}), bf16[4,144,1024]{2,1,0:T(8,128)(2,1)S(1)}, u32[]{:S(2)}, u32[]{:S(2)}) %all-to-all-start.1) | async-done | bytes 1179680 | tf_op jit(solution)/shard_map/all_to_all | solution.py:215
  36.7 3.5 %all-to-all-start = ((bf16[4,144,1024]{2,1,0:T(8,128)(2,1)}), bf16[4,144,1024]{2,1,0:T(8,128)(2,1)S(1)}, u32[]{:S(2)}, u32[]{:S(2)}) async-start(bf16[4,144,1024]{2,1,0:T(8,128)(2,1)} %maximum_bitcast_fusion), calls=%async_computation | async-start | bytes 2359296 | tf_op jit(solution)/shard_map/all_to_all | solution.py:215
  40.2 0.1 copy.25
  40.3 0.1 reshape.60.send_ref
  40.4 0.7 dynamic-slice_bitcast_fusion.table_ref
  41.1 1.7 %lend.1 = (bf16[192,1024]{1,0:T(8,128)(2,1)}, bf16[192,1024]{1,0:T(8,128)(2,1)}, bf16[192,1024]{1,0:T(8,128)(2,1)}, bf16[64,1024]{1,0:T(8,128)(2,1)}, bf16[64,1024]{1,0:T(8,128)(2,1)}) custom-call(s32[43]{0:T(128)S(1)} %dynamic-slice_bitcast_fusion.table_ref, s32[24]{0:T(128)S(1)} %reshape.60.send_ref, bf16[576,1024]{1,0:T(8,128)(2,1)S(1)} %bitcast.37), custom_call_target="tpu_custom_call" | custom-call | tf_op jit(solution)/shard_map/lend/pallas_call | solution.py:230
  42.8 3.4 %collective-permute-start = (bf16[192,1024]{1,0:T(8,128)(2,1)}, bf16[192,1024]{1,0:T(8,128)(2,1)S(1)}, u32[]{:S(2)}, u32[]{:S(2)}) collective-permute-start(bf16[192,1024]{1,0:T(8,128)(2,1)} %get-tuple-element.15), channel_id=1, source_target_pairs={{0,8},{4,12},{8,16},{12,20},{16,24},{20,28},{1,9},{5,13},{9,17},{1... | collective-permute-start | bytes 1179656 | tf_op jit(solution)/shard_map/ppermute | solution.py:238
  46.2 0.1 collective-permute-start.1
  46.3 3.3 %collective-permute-start.2 = (bf16[192,1024]{1,0:T(8,128)(2,1)}, bf16[192,1024]{1,0:T(8,128)(2,1)S(1)}, u32[]{:S(2)}, u32[]{:S(2)}) collective-permute-start(bf16[192,1024]{1,0:T(8,128)(2,1)} %get-tuple-element.17), channel_id=1, source_target_pairs={{8,0},{12,4},{16,8},{20,12},{24,16},{28,20},{9,1},{13,5},{17,9},{2... | collective-permute-start | bytes 1179656 | tf_op jit(solution)/shard_map/ppermute | solution.py:238
  49.6 2.3 %collective-permute-start.3 = (bf16[64,1024]{1,0:T(8,128)(2,1)}, bf16[64,1024]{1,0:T(8,128)(2,1)}, u32[]{:S(2)}, u32[]{:S(2)}) collective-permute-start(bf16[64,1024]{1,0:T(8,128)(2,1)} %get-tuple-element.18), channel_id=1, source_target_pairs={{0,12},{8,20},{16,28},{4,8},{12,16},{20,24},{1,13},{9,21},{17,29},... | collective-permute-start | bytes 393224 | tf_op jit(solution)/shard_map/ppermute | solution.py:238
  52.0 4.1 %collective-permute-start.4 = (bf16[64,1024]{1,0:T(8,128)(2,1)}, bf16[64,1024]{1,0:T(8,128)(2,1)}, u32[]{:S(2)}, u32[]{:S(2)}) collective-permute-start(bf16[64,1024]{1,0:T(8,128)(2,1)} %get-tuple-element.19), channel_id=1, source_target_pairs={{8,4},{16,12},{24,20},{12,0},{20,8},{28,16},{9,5},{17,13},{25,21},... | collective-permute-start | bytes 393224 | tf_op jit(solution)/shard_map/ppermute | solution.py:238
  56.1 0.8 reshape.51.near_ref
  56.9 2.7 %copy.26.bias_ref = f32[576,512]{1,0:T(8,128)} copy(f32[576,512]{0,1:T(8,128)} %bitcast.42) | data formatting | bytes 2359296 | tf_op jit(solution)/shard_map/reshape | solution.py:227
  59.6 8.6 %all-to-all-done = bf16[4,144,1024]{2,1,0:T(8,128)(2,1)S(1)} async-done(((bf16[4,144,1024]{2,1,0:T(8,128)(2,1)}), bf16[4,144,1024]{2,1,0:T(8,128)(2,1)S(1)}, u32[]{:S(2)}, u32[]{:S(2)}) %all-to-all-start) | async-done | bytes 1179680 | tf_op jit(solution)/shard_map/all_to_all | solution.py:215
  68.2 0.0 collective-permute-done.3.refs_3_
  68.2 0.0 collective-permute-done.4.refs_4_
  68.2 0.0 collective-permute-done.refs_0_
  68.2 0.0 collective-permute-done.1.refs_1_
  68.2 0.0 collective-permute-done.2.refs_2_
  68.3 0.0 copy-start.3
  68.3 0.7 copy-done.3
  69.0 1.0 copy-done.4
  70.0 22.0 %attend.1 = (bf16[576,512]{1,0:T(8,128)(2,1)}, f32[576,1024]{1,0:T(8,128)}, bf16[192,1024]{1,0:T(8,128)(2,1)S(1)}, bf16[192,1024]{1,0:T(8,128)(2,1)S(1)}, bf16[1...) custom-call(s32[43]{0:T(128)S(1)} %dynamic-slice_bitcast_fusion.table_ref, ...), custom_call_target="tpu_custom_call" | custom-call | flops 1698693120 | bytes 2359296 | tf_op jit(solution)/shard_map/attend/pallas_call | solution.py:240
  92.0 0.7 copy-done.1
  92.7 0.7 copy-done.5
  93.5 0.7 copy-done.7
  94.1 0.6 copy-done.9
  94.8 4.8 %all-to-all-start.2 = ((bf16[4,144,512]{2,1,0:T(8,128)(2,1)}), bf16[4,144,512]{2,1,0:T(8,128)(2,1)S(1)}, u32[]{:S(2)}, u32[]{:S(2)}) async-start(bf16[4,144,512]{2,1,0:T(8,128)(2,1)} %bitcast.8), calls=%async_computation.2 | async-start | bytes 1179648 | tf_op jit(solution)/shard_map/all_to_all | solution.py:220
  99.6 3.3 %collective-permute-start.5 = (bf16[192,1024]{1,0:T(8,128)(2,1)S(1)}, bf16[192,1024]{1,0:T(8,128)(2,1)S(1)}, u32[]{:S(2)}, u32[]{:S(2)}) collective-permute-start(bf16[192,1024]{1,0:T(8,128)(2,1)S(1)} %copy-done.6), channel_id=1, source_target_pairs={{8,0},{12,4},{16,8},{20,12},{24,16},{28,20},{9,1},{13,5},{17,9},{2... | collective-permute-start | bytes 1179656 | tf_op jit(solution)/shard_map/ppermute | solution.py:257
  102.9 1.3 collective-permute-start.6
  104.2 1.9 %collective-permute-start.7 = (bf16[192,1024]{1,0:T(8,128)(2,1)S(1)}, bf16[192,1024]{1,0:T(8,128)(2,1)S(1)}, u32[]{:S(2)}, u32[]{:S(2)}) collective-permute-start(bf16[192,1024]{1,0:T(8,128)(2,1)S(1)} %get-tuple-element.24), channel_id=1, source_target_pairs={{0,8},{4,12},{8,16},{12,20},{16,24},{20,28},{1,9},{5,13},{9,17},{1... | collective-permute-start | bytes 1179656 | tf_op jit(solution)/shard_map/ppermute | solution.py:257
  106.1 4.2 %collective-permute-start.8 = (bf16[64,1024]{1,0:T(8,128)(2,1)S(1)}, bf16[64,1024]{1,0:T(8,128)(2,1)S(1)}, u32[]{:S(2)}, u32[]{:S(2)}) collective-permute-start(bf16[64,1024]{1,0:T(8,128)(2,1)S(1)} %copy-done.10), channel_id=1, source_target_pairs={{12,0},{20,8},{28,16},{8,4},{16,12},{24,20},{13,1},{21,9},{29,17},... | collective-permute-start | bytes 393224 | tf_op jit(solution)/shard_map/ppermute | solution.py:257
  110.3 1.9 %collective-permute-start.9 = (bf16[64,1024]{1,0:T(8,128)(2,1)S(1)}, bf16[64,1024]{1,0:T(8,128)(2,1)S(1)}, u32[]{:S(2)}, u32[]{:S(2)}) collective-permute-start(bf16[64,1024]{1,0:T(8,128)(2,1)S(1)} %copy-done.8), channel_id=1, source_target_pairs={{4,8},{12,16},{20,24},{0,12},{8,20},{16,28},{5,9},{13,17},{21,25},... | collective-permute-start | bytes 393224 | tf_op jit(solution)/shard_map/ppermute | solution.py:257
  112.3 10.9 %collective-permute-done.8.refs_3_ = bf16[64,1024]{1,0:T(8,128)(2,1)S(1)} collective-permute-done((bf16[64,1024]{1,0:T(8,128)(2,1)S(1)}, bf16[64,1024]{1,0:T(8,128)(2,1)S(1)}, u32[]{:S(2)}, u32[]{:S(2)}) %collective-permute-start.8) | collective-permute-done | bytes 131104 | tf_op jit(solution)/shard_map/ppermute | solution.py:257
  123.2 4.0 %collective-permute-done.9.refs_4_ = bf16[64,1024]{1,0:T(8,128)(2,1)S(1)} collective-permute-done((bf16[64,1024]{1,0:T(8,128)(2,1)S(1)}, bf16[64,1024]{1,0:T(8,128)(2,1)S(1)}, u32[]{:S(2)}, u32[]{:S(2)}) %collective-permute-start.9) | collective-permute-done | bytes 131104 | tf_op jit(solution)/shard_map/ppermute | solution.py:257
  127.2 1.7 copy-done
  128.8 2.1 %settle.1 = bf16[576,1024]{1,0:T(8,128)(2,1)} custom-call(s32[43]{0:T(128)S(1)} %dynamic-slice_bitcast_fusion.table_ref, s32[24]{0:T(128)S(1)} %reshape.60.send_ref, f32[576,1024]{1,0:T(8,128)S(1)} %copy-done, bf16[192,1024]{1,0:T(8,128)(2,1)S(1)} %collective-permute-done.5.refs_0_, bf16[192,1024]{1,0:T(8,128)(2,1)S(1)} %collective-permute-done.6.refs_1_, ...), custom_call_target="tpu_custom_call" | custom-call | tf_op jit(solution)/shard_map/settle/pallas_call | solution.py:260
  130.9 5.1 %all-to-all-start.3 = ((bf16[4,144,1024]{2,1,0:T(8,128)(2,1)}), bf16[4,144,1024]{2,1,0:T(8,128)(2,1)S(1)}, u32[]{:S(2)}, u32[]{:S(2)}) async-start(bf16[4,144,1024]{2,1,0:T(8,128)(2,1)} %bitcast.10), calls=%async_computation.3 | async-start | bytes 2359296 | tf_op jit(solution)/shard_map/all_to_all | solution.py:220
  136.0 0.9 copy.34
  136.9 27.4 %all-to-all-done.3 = bf16[4,144,1024]{2,1,0:T(8,128)(2,1)S(1)} async-done(((bf16[4,144,1024]{2,1,0:T(8,128)(2,1)}), bf16[4,144,1024]{2,1,0:T(8,128)(2,1)S(1)}, u32[]{:S(2)}, u32[]{:S(2)}) %all-to-all-start.3) | async-done | bytes 1179680 | tf_op jit(solution)/shard_map/all_to_all | solution.py:220
  164.4 0.1 slice_bitcast_fusion
  164.5 0.9 copy.36
  165.4 0.9 copy.35
  (26 shorter events, 0.0 us)
Async XLA Ops:
  3.1 5.0 %copy-start.12 = (bf16[144,2048]{1,0:T(8,128)(2,1)S(1)}, bf16[144,2048]{1,0:T(8,128)(2,1)}, u32[]{:S(2)}) copy-start(bf16[144,2048]{1,0:T(8,128)(2,1)} %param.12) | copy-start | bytes 1769476
  3.1 5.0 %copy-start.13 = (bf16[144,2048]{1,0:T(8,128)(2,1)S(1)}, bf16[144,2048]{1,0:T(8,128)(2,1)}, u32[]{:S(2)}) copy-start(bf16[144,2048]{1,0:T(8,128)(2,1)} %param.9) | copy-start | bytes 1769476
  3.1 33.5 %all-to-all-start.1 = ((bf16[4,144,1024]{2,1,0:T(8,128)(2,1)}), bf16[4,144,1024]{2,1,0:T(8,128)(2,1)S(1)}, u32[]{:S(2)}, u32[]{:S(2)}) async-start(bf16[4,144,1024]{2,1,0:T(8,128)(2,1)} %maximum_bitcast_fusion.1), calls=%async_computation.1 | async-start | bytes 2359296 | tf_op jit(solution)/shard_map/all_to_all | solution.py:215
  9.4 30.8 %copy-start.14 = (s32[1,8,3]{1,0,2:T(1,128)S(1)}, s32[1,8,3]{1,0,2:T(1,128)}, u32[]{:S(2)}) copy-start(s32[1,8,3]{1,0,2:T(1,128)} %param.15) | copy-start | bytes 292
  36.7 31.5 %all-to-all-start = ((bf16[4,144,1024]{2,1,0:T(8,128)(2,1)}), bf16[4,144,1024]{2,1,0:T(8,128)(2,1)S(1)}, u32[]{:S(2)}, u32[]{:S(2)}) async-start(bf16[4,144,1024]{2,1,0:T(8,128)(2,1)} %maximum_bitcast_fusion), calls=%async_computation | async-start | bytes 2359296 | tf_op jit(solution)/shard_map/all_to_all | solution.py:215
  42.8 25.4 %collective-permute-start = (bf16[192,1024]{1,0:T(8,128)(2,1)}, bf16[192,1024]{1,0:T(8,128)(2,1)S(1)}, u32[]{:S(2)}, u32[]{:S(2)}) collective-permute-start(bf16[192,1024]{1,0:T(8,128)(2,1)} %get-tuple-element.15), channel_id=1, source_target_pairs={{0,8},{4,12},{8,16},{12,20},{16,24},{20,28},{1,9},{5,13},{9,17},{1... | collective-permute-start | bytes 1179656 | tf_op jit(solution)/shard_map/ppermute | solution.py:238
  46.2 22.0 %collective-permute-start.1 = (bf16[192,1024]{1,0:T(8,128)(2,1)}, bf16[192,1024]{1,0:T(8,128)(2,1)S(1)}, u32[]{:S(2)}, u32[]{:S(2)}) collective-permute-start(bf16[192,1024]{1,0:T(8,128)(2,1)} %get-tuple-element.16), channel_id=1, source_target_pairs={{0,4},{8,12},{16,20},{24,28},{4,0},{12,8},{20,16},{28,24},{1,5},{9... | collective-permute-start | bytes 1179656 | tf_op jit(solution)/shard_map/ppermute | solution.py:238
  46.3 22.0 %collective-permute-start.2 = (bf16[192,1024]{1,0:T(8,128)(2,1)}, bf16[192,1024]{1,0:T(8,128)(2,1)S(1)}, u32[]{:S(2)}, u32[]{:S(2)}) collective-permute-start(bf16[192,1024]{1,0:T(8,128)(2,1)} %get-tuple-element.17), channel_id=1, source_target_pairs={{8,0},{12,4},{16,8},{20,12},{24,16},{28,20},{9,1},{13,5},{17,9},{2... | collective-permute-start | bytes 1179656 | tf_op jit(solution)/shard_map/ppermute | solution.py:238
  49.6 18.6 %collective-permute-start.3 = (bf16[64,1024]{1,0:T(8,128)(2,1)}, bf16[64,1024]{1,0:T(8,128)(2,1)}, u32[]{:S(2)}, u32[]{:S(2)}) collective-permute-start(bf16[64,1024]{1,0:T(8,128)(2,1)} %get-tuple-element.18), channel_id=1, source_target_pairs={{0,12},{8,20},{16,28},{4,8},{12,16},{20,24},{1,13},{9,21},{17,29},... | collective-permute-start | bytes 393224 | tf_op jit(solution)/shard_map/ppermute | solution.py:238
  52.0 16.2 %collective-permute-start.4 = (bf16[64,1024]{1,0:T(8,128)(2,1)}, bf16[64,1024]{1,0:T(8,128)(2,1)}, u32[]{:S(2)}, u32[]{:S(2)}) collective-permute-start(bf16[64,1024]{1,0:T(8,128)(2,1)} %get-tuple-element.19), channel_id=1, source_target_pairs={{8,4},{16,12},{24,20},{12,0},{20,8},{28,16},{9,5},{17,13},{25,21},... | collective-permute-start | bytes 393224 | tf_op jit(solution)/shard_map/ppermute | solution.py:238
  56.9 12.1 %copy-start.11 = (s32[1,8]{1,0:T(1,128)S(1)}, s32[1,8]{1,0:T(1,128)}, u32[]{:S(2)}) copy-start(s32[1,8]{1,0:T(1,128)} %param.16) | copy-start | bytes 100
  68.3 0.7 copy-start.3
  69.0 1.0 copy-start.4
  92.0 0.7 copy-start.1
  92.7 0.7 copy-start.5
  93.5 0.7 copy-start.7
  94.1 0.6 copy-start.9
  94.8 4.8 %copy-start.6 = (bf16[192,1024]{1,0:T(8,128)(2,1)S(1)}, bf16[192,1024]{1,0:T(8,128)(2,1)}, u32[]{:S(2)}) copy-start(bf16[192,1024]{1,0:T(8,128)(2,1)} %copy-done.5) | copy-start | bytes 1179652
  94.8 8.2 %copy-start.2 = (bf16[192,1024]{1,0:T(8,128)(2,1)S(1)}, bf16[192,1024]{1,0:T(8,128)(2,1)}, u32[]{:S(2)}) copy-start(bf16[192,1024]{1,0:T(8,128)(2,1)} %copy-done.1) | copy-start | bytes 1179652
  94.8 11.4 %copy-start.10 = (bf16[64,1024]{1,0:T(8,128)(2,1)S(1)}, bf16[64,1024]{1,0:T(8,128)(2,1)}, u32[]{:S(2)}) copy-start(bf16[64,1024]{1,0:T(8,128)(2,1)} %copy-done.9) | copy-start | bytes 393220
  94.8 15.6 %copy-start.8 = (bf16[64,1024]{1,0:T(8,128)(2,1)S(1)}, bf16[64,1024]{1,0:T(8,128)(2,1)}, u32[]{:S(2)}) copy-start(bf16[64,1024]{1,0:T(8,128)(2,1)} %copy-done.7) | copy-start | bytes 393220
  94.8 36.2 %all-to-all-start.2 = ((bf16[4,144,512]{2,1,0:T(8,128)(2,1)}), bf16[4,144,512]{2,1,0:T(8,128)(2,1)S(1)}, u32[]{:S(2)}, u32[]{:S(2)}) async-start(bf16[4,144,512]{2,1,0:T(8,128)(2,1)} %bitcast.8), calls=%async_computation.2 | async-start | bytes 1179648 | tf_op jit(solution)/shard_map/all_to_all | solution.py:220
  99.6 27.5 %collective-permute-start.5 = (bf16[192,1024]{1,0:T(8,128)(2,1)S(1)}, bf16[192,1024]{1,0:T(8,128)(2,1)S(1)}, u32[]{:S(2)}, u32[]{:S(2)}) collective-permute-start(bf16[192,1024]{1,0:T(8,128)(2,1)S(1)} %copy-done.6), channel_id=1, source_target_pairs={{8,0},{12,4},{16,8},{20,12},{24,16},{28,20},{9,1},{13,5},{17,9},{2... | collective-permute-start | bytes 1179656 | tf_op jit(solution)/shard_map/ppermute | solution.py:257
  102.9 24.2 %collective-permute-start.6 = (bf16[192,1024]{1,0:T(8,128)(2,1)S(1)}, bf16[192,1024]{1,0:T(8,128)(2,1)S(1)}, u32[]{:S(2)}, u32[]{:S(2)}) collective-permute-start(bf16[192,1024]{1,0:T(8,128)(2,1)S(1)} %copy-done.2), channel_id=1, source_target_pairs={{4,0},{12,8},{20,16},{28,24},{0,4},{8,12},{16,20},{24,28},{5,1},{1... | collective-permute-start | bytes 1179656 | tf_op jit(solution)/shard_map/ppermute | solution.py:257
  104.2 22.9 %collective-permute-start.7 = (bf16[192,1024]{1,0:T(8,128)(2,1)S(1)}, bf16[192,1024]{1,0:T(8,128)(2,1)S(1)}, u32[]{:S(2)}, u32[]{:S(2)}) collective-permute-start(bf16[192,1024]{1,0:T(8,128)(2,1)S(1)} %get-tuple-element.24), channel_id=1, source_target_pairs={{0,8},{4,12},{8,16},{12,20},{16,24},{20,28},{1,9},{5,13},{9,17},{1... | collective-permute-start | bytes 1179656 | tf_op jit(solution)/shard_map/ppermute | solution.py:257
  106.1 17.0 %collective-permute-start.8 = (bf16[64,1024]{1,0:T(8,128)(2,1)S(1)}, bf16[64,1024]{1,0:T(8,128)(2,1)S(1)}, u32[]{:S(2)}, u32[]{:S(2)}) collective-permute-start(bf16[64,1024]{1,0:T(8,128)(2,1)S(1)} %copy-done.10), channel_id=1, source_target_pairs={{12,0},{20,8},{28,16},{8,4},{16,12},{24,20},{13,1},{21,9},{29,17},... | collective-permute-start | bytes 393224 | tf_op jit(solution)/shard_map/ppermute | solution.py:257
  110.3 16.8 %collective-permute-start.9 = (bf16[64,1024]{1,0:T(8,128)(2,1)S(1)}, bf16[64,1024]{1,0:T(8,128)(2,1)S(1)}, u32[]{:S(2)}, u32[]{:S(2)}) collective-permute-start(bf16[64,1024]{1,0:T(8,128)(2,1)S(1)} %copy-done.8), channel_id=1, source_target_pairs={{4,8},{12,16},{20,24},{0,12},{8,20},{16,28},{5,9},{13,17},{21,25},... | collective-permute-start | bytes 393224 | tf_op jit(solution)/shard_map/ppermute | solution.py:257
  127.1 1.7 %copy-start = (f32[576,1024]{1,0:T(8,128)S(1)}, f32[576,1024]{1,0:T(8,128)}, u32[]{:S(2)}) copy-start(f32[576,1024]{1,0:T(8,128)} %get-tuple-element.21.own_ref) | copy-start | bytes 7077892
  130.9 33.4 %all-to-all-start.3 = ((bf16[4,144,1024]{2,1,0:T(8,128)(2,1)}), bf16[4,144,1024]{2,1,0:T(8,128)(2,1)S(1)}, u32[]{:S(2)}, u32[]{:S(2)}) async-start(bf16[4,144,1024]{2,1,0:T(8,128)(2,1)} %bitcast.10), calls=%async_computation.3 | async-start | bytes 2359296 | tf_op jit(solution)/shard_map/all_to_all | solution.py:220
